TPU v7x, 32 devices: a whole 2x2x4 slice. The times are simulated.
32 devices in a mesh: grp: 2 (over y), bx: 4 (over z), by: 4 (over x, core).
Axes of the slice: x: 2, y: 2, z: 4, core: 2. Of those that a mesh axis runs over, the one named last changes fastest.
Arguments:
- psi: float32 [121, 4, 4, 256], P(None, 'bx', 'by', 'grp'), parts along dimension 3
- nbr_block: int32 [4, 4, 32, 256], P('bx', 'by', None, 'grp'), parts along dimension 3, may hold values from 0 to 8, as said below
- nbr_sphere: int32 [4, 4, 32, 256], P('bx', 'by', None, 'grp'), parts along dimension 3, may hold values from 0 to 127
- counts: int32 [4, 4, 256], P('bx', 'by', 'grp'), parts along dimension 2, may hold values from 1 to 32, as said below
- couple: bfloat16 [302, 4, 4, 32, 256], P(None, 'bx', 'by', None, 'grp'), parts along dimension 4, may hold values from 0.135 to 0.25
- ratio: float32 [4, 4, 32, 256], P('bx', 'by', None, 'grp'), parts along dimension 3, may hold values from 0.75 to 0.85
Outputs:
- solution: float32 [121, 4, 4, 256], P(None, 'bx', 'by', 'grp'), parts along dimension 3
- step_norms: float32 [6], P('grp'), parts along dimension 0
There are 2 independent parts, one for each index of `grp`. A program takes and returns all parts, laid end to end along the dimension named above; each array names one. Nothing has to cross between parts.
Inputs may be any that keep to these rules, and one draw needn't show every extreme that they name: `nbr_block`: every named block lies inside the grid of blocks. `counts`: in every block some sphere uses the block's largest count, which lies between 16 and 32; in some block it is all 32.
All inputs are finite; a program needn't handle non-finite values.
Results may differ from a plain program's by a relative error of at most 0.0003.
Values sent between devices are 32-bit elements; how exact they have to be, the bound alone decides.
A program may use at most 64 MiB of HBM per device.

v0:
```python
import functools
import math

import jax
import jax.numpy as jnp
import numpy as np
from jax import lax
from jax.experimental import pallas as pl
from jax.experimental.pallas import tpu as pltpu
from jax.sharding import PartitionSpec as P

SWEEPS = 3
MESH = pl.DeviceIdType.MESH
GOLDEN = 2.399963229728653
HP = 128
WIDE = 2
BF = jnp.bfloat16
F32 = jnp.float32


def basis_table(npts, lmax):
    index = np.arange(npts, dtype=np.float64)
    zval = 1.0 - (2.0 * index + 1.0) / npts
    sinval = np.sqrt(np.maximum(1.0 - zval * zval, 0.0))
    angle = GOLDEN * index
    table = {(0, 0): np.full((npts,), 1.0 / math.sqrt(4.0 * math.pi))}
    for order in range(1, lmax + 1):
        table[order, order] = (
            -math.sqrt((2.0 * order + 1.0) / (2.0 * order)) * sinval * table[order - 1, order - 1]
        )
    for order in range(0, lmax):
        table[order + 1, order] = math.sqrt(2.0 * order + 3.0) * zval * table[order, order]
    for order in range(0, lmax + 1):
        for degree in range(order + 2, lmax + 1):
            first = math.sqrt((4.0 * degree * degree - 1.0) / (degree * degree - order * order))
            second = math.sqrt(
                ((degree - 1.0) ** 2 - order * order) / (4.0 * (degree - 1.0) ** 2 - 1.0)
            )
            table[degree, order] = first * (
                zval * table[degree - 1, order] - second * table[degree - 2, order]
            )
    columns = []
    for degree in range(lmax + 1):
        for order in range(-degree, degree + 1):
            if order < 0:
                columns.append(math.sqrt(2.0) * table[degree, -order] * np.sin(-order * angle))
            elif order == 0:
                columns.append(table[degree, 0])
            else:
                columns.append(math.sqrt(2.0) * table[degree, order] * np.cos(order * angle))
    return np.stack(columns, axis=1)


def split_np(x):
    hi = x.astype(np.float32).astype(BF)
    lo = (x - hi.astype(np.float64)).astype(np.float32).astype(BF)
    return hi, lo


def kernel(
    nbx, nby, cells,
    psi_ref, nblk_ref, nsph_ref, cnt_ref, couple_ref, ratio_ref, bc_ref, bt_ref, deg_ref, invd_ref,
    out_ref, norm_ref,
    cin, cf, cd, onehot, power, land, solcat, sol0, nb, nland1, nland2,
    csem, ssem, rsem, s1, r1, s2, r2,
):
    lh, sph = psi_ref.shape
    npts, slots, _ = couple_ref.shape
    npad = bc_ref.shape[0]
    groups = slots // WIDE
    wide = WIDE * sph
    ix, iy, ig = lax.axis_index("bx"), lax.axis_index("by"), lax.axis_index("grp")

    copy_in = pltpu.make_async_copy(couple_ref, cin, csem)
    copy_in.start()

    dirs = [d for d in range(9) if d != 4]
    inside = {}
    for d in dirs:
        tx, ty = ix + d // 3 - 1, iy + d % 3 - 1
        inside[d] = (tx >= 0) & (tx < nbx) & (ty >= 0) & (ty < nby)

    def device(d):
        return (ig, ix + d // 3 - 1, iy + d % 3 - 1)

    barrier = pltpu.get_barrier_semaphore()
    count = jnp.int32(0)
    for d in dirs:
        count = count + inside[d].astype(jnp.int32)

        @pl.when(inside[d])
        def _(d=d):
            pl.semaphore_signal(barrier, inc=1, device_id=device(d), device_id_type=MESH)

    for off in range(1, nby):
        peer = lax.rem(iy + off, nby)
        far = jnp.abs(peer - iy) >= 2
        count = count + far.astype(jnp.int32)

        @pl.when(far)
        def _(peer=peer):
            pl.semaphore_signal(barrier, inc=1, device_id=(ig, ix, peer), device_id_type=MESH)

    for off in range(1, nbx):
        peer = lax.rem(ix + off, nbx)
        far = jnp.abs(peer - ix) >= 2
        count = count + far.astype(jnp.int32)

        @pl.when(far)
        def _(peer=peer):
            pl.semaphore_signal(barrier, inc=1, device_id=(ig, peer, iy), device_id_type=MESH)

    sol0[...] = jnp.zeros_like(sol0)
    sol0[pl.ds(0, lh), :] = psi_ref[...] * invd_ref[pl.ds(0, lh), :]
    land[0, 4] = sol0[...]
    pl.semaphore_wait(barrier, count)

    def block_copy(t, d):
        return pltpu.make_async_remote_copy(
            src_ref=land.at[t, 4],
            dst_ref=land.at[t, 8 - d],
            send_sem=ssem.at[t, d],
            recv_sem=rsem.at[t, 8 - d],
            device_id=device(d),
            device_id_type=MESH,
        )

    def block_arrival(t, d):
        return pltpu.make_async_remote_copy(
            src_ref=land.at[t, 4],
            dst_ref=land.at[t, d],
            send_sem=ssem.at[t, d],
            recv_sem=rsem.at[t, d],
            device_id=device(d),
            device_id_type=MESH,
        )

    def send_all(t):
        for d in dirs:
            @pl.when(inside[d])
            def _(d=d):
                block_copy(t, d).start()

    def place(block, d):
        hi = block.astype(BF)
        lo = (block - hi.astype(F32)).astype(BF)
        solcat[pl.ds(0, HP), pl.ds(d * sph, sph)] = hi
        solcat[pl.ds(HP, HP), pl.ds(d * sph, sph)] = lo

    send_all(0)

    rows = lax.broadcasted_iota(jnp.int32, (9 * sph, sph), 0)

    def prepare(g, carry):
        for w in range(WIDE):
            s = g * WIDE + w
            lanes = pl.ds(w * sph, sph)
            index = nblk_ref[pl.ds(s, 1), :] * sph + nsph_ref[pl.ds(s, 1), :]
            onehot[g, :, lanes] = (rows == index).astype(F32).astype(BF)
            logr = jnp.log(ratio_ref[pl.ds(s, 1), :])
            raised = jnp.exp(deg_ref[...] * logr) * invd_ref[...]
            power[g, :, lanes] = jnp.where(s < cnt_ref[...], raised, 0.0)
        return carry

    lax.fori_loop(0, groups, prepare, 0)

    copy_in.wait()

    def widen(n, carry):
        cf[pl.ds(n * slots, slots), :] = cin[n].astype(F32)
        return carry

    lax.fori_loop(0, npts, widen, 0, unroll=2)
    cf[pl.ds(npts * slots, (npad - npts) * slots), :] = jnp.zeros(((npad - npts) * slots, sph), F32)

    def turn(g, carry):
        for w in range(WIDE):
            cd[g, :, pl.ds(w * sph, sph)] = cf[pl.ds(g * WIDE + w, npad, stride=slots), :]
        return carry

    lax.fori_loop(0, groups, turn, 0)

    nb[...] = jnp.zeros_like(nb)
    for t in range(SWEEPS):
        old = land[t, 4]
        place(old, 4)
        for d in dirs:
            @pl.when(inside[d])
            def _(d=d, t=t):
                block_arrival(t, d).wait_recv()
                place(land[t, d], d)

            if t == 0:
                @pl.when(jnp.logical_not(inside[d]))
                def _(d=d):
                    solcat[:, pl.ds(d * sph, sph)] = jnp.zeros((2 * HP, sph), BF)

        def pairs(g, total):
            picked = jnp.dot(solcat[...], onehot[g], preferred_element_type=F32).astype(BF)
            stacked = jnp.concatenate([picked, picked[:HP]], axis=0)
            points = jnp.dot(bc_ref[...], stacked, preferred_element_type=F32)
            product = points * cd[g]
            hi = product.astype(BF)
            lo = (product - hi.astype(F32)).astype(BF)
            back = jnp.dot(
                bt_ref[...], jnp.concatenate([hi, lo, hi], axis=0), preferred_element_type=F32
            )
            terms = back * power[g]
            for w in range(WIDE):
                total = total + terms[:, w * sph:(w + 1) * sph]
            return total

        total = lax.fori_loop(0, groups, pairs, jnp.zeros((HP, sph), F32), unroll=2)
        fresh = sol0[...] - total
        if t < SWEEPS - 1:
            land[t + 1, 4] = fresh
            send_all(t + 1)
        else:
            out_ref[...] = fresh[:lh]
        nb[pl.ds(t, 1), :] = jnp.sum((fresh - old) ** 2, axis=0, keepdims=True)

    def reduce_line(mine, slots_ref, send, recv, me, count, where):
        slots_ref[me] = mine
        copies = []
        for off in range(1, count):
            peer = lax.rem(me + off, count)
            copy = pltpu.make_async_remote_copy(
                src_ref=slots_ref.at[me],
                dst_ref=slots_ref.at[me],
                send_sem=send.at[off],
                recv_sem=recv.at[me],
                device_id=where(peer),
                device_id_type=MESH,
            )
            copy.start()
            copies.append(copy)
        for off in range(1, count):
            peer = lax.rem(me + off, count)
            pltpu.make_async_remote_copy(
                src_ref=slots_ref.at[me],
                dst_ref=slots_ref.at[peer],
                send_sem=send.at[off],
                recv_sem=recv.at[peer],
                device_id=where(peer),
                device_id_type=MESH,
            ).wait_recv()
        result = slots_ref[0]
        for i in range(1, count):
            result = result + slots_ref[i]
        for copy in copies:
            copy.wait_send()
        return result

    part = reduce_line(nb[...], nland1, s1, r1, iy, nby, lambda p: (ig, ix, p))
    part = reduce_line(part, nland2, s2, r2, ix, nbx, lambda p: (ig, p, iy))
    norm = jnp.sqrt(jnp.sum(part, axis=1, keepdims=True) * (1.0 / cells))
    norm_ref[...] = jnp.broadcast_to(norm, norm_ref.shape)

    for t in range(SWEEPS):
        for d in dirs:
            @pl.when(inside[d])
            def _(d=d, t=t):
                block_copy(t, d).wait_send()


def on_device(nbx, nby, psi, nbr_block, nbr_sphere, counts, couple, ratio):
    lh, sph = psi.shape[0], psi.shape[3]
    slots = nbr_block.shape[2]
    npts = couple.shape[0]
    lmax = math.isqrt(lh) - 1
    npad = -(-npts // 16) * 16
    basis = np.zeros((npad, HP))
    basis[:npts, :lh] = basis_table(npts, lmax)
    degrees = np.zeros((HP,))
    degrees[:lh] = np.repeat(np.arange(lmax + 1), 2 * np.arange(lmax + 1) + 1)
    inverse = (2.0 * degrees + 1.0) / (4.0 * math.pi)
    inverse[lh:] = 0.0
    hi, lo = split_np(basis * (4.0 * math.pi / npts))
    bc = np.concatenate([hi, hi, lo], axis=1)
    hi, lo = split_np(basis.T)
    bt = np.concatenate([hi, hi, lo], axis=1)
    deg = np.broadcast_to(degrees[:, None], (HP, sph)).astype(np.float32)
    invd = np.broadcast_to(inverse[:, None], (HP, sph)).astype(np.float32)
    cells = lh * sph * nbx * nby
    groups = slots // WIDE
    vmem = pl.BlockSpec(memory_space=pltpu.VMEM)
    out, norms = pl.pallas_call(
        functools.partial(kernel, nbx, nby, cells),
        out_shape=(
            jax.ShapeDtypeStruct((lh, sph), F32),
            jax.ShapeDtypeStruct((8, 128), F32),
        ),
        in_specs=[vmem] * 4 + [pl.BlockSpec(memory_space=pl.ANY)] + [vmem] * 5,
        out_specs=(vmem, vmem),
        scratch_shapes=[
            pltpu.VMEM((npts, slots, sph), BF),
            pltpu.VMEM((npad * slots, sph), F32),
            pltpu.VMEM((groups, npad, WIDE * sph), F32),
            pltpu.VMEM((groups, 9 * sph, WIDE * sph), BF),
            pltpu.VMEM((groups, HP, WIDE * sph), F32),
            pltpu.VMEM((SWEEPS, 9, HP, sph), F32),
            pltpu.VMEM((2 * HP, 9 * sph), BF),
            pltpu.VMEM((HP, sph), F32),
            pltpu.VMEM((8, sph), F32),
            pltpu.VMEM((nby, 8, sph), F32),
            pltpu.VMEM((nbx, 8, sph), F32),
            pltpu.SemaphoreType.DMA(()),
            pltpu.SemaphoreType.DMA((SWEEPS, 9)),
            pltpu.SemaphoreType.DMA((SWEEPS, 9)),
            pltpu.SemaphoreType.DMA((nby,)),
            pltpu.SemaphoreType.DMA((nby,)),
            pltpu.SemaphoreType.DMA((nbx,)),
            pltpu.SemaphoreType.DMA((nbx,)),
        ],
        compiler_params=pltpu.CompilerParams(
            collective_id=0, has_side_effects=True, vmem_limit_bytes=48 * 1024 * 1024
        ),
        cost_estimate=pl.CostEstimate(
            flops=2 * SWEEPS * slots * sph * (2304 * HP + 6 * npad * HP),
            bytes_accessed=4 * 1024 * 1024,
            transcendentals=slots * sph * HP,
        ),
    )(
        psi.reshape(lh, sph),
        nbr_block.reshape(slots, sph),
        nbr_sphere.reshape(slots, sph),
        counts.reshape(1, sph),
        couple.reshape(npts, slots, sph),
        ratio.reshape(slots, sph),
        jnp.asarray(bc),
        jnp.asarray(bt),
        jnp.asarray(deg),
        jnp.asarray(invd),
    )
    return out.reshape(lh, 1, 1, sph), norms[:SWEEPS, 0]


def solution(mesh):
    return jax.shard_map(
        functools.partial(on_device, mesh.shape["bx"], mesh.shape["by"]),
        mesh=mesh,
        in_specs=(
            P(None, "bx", "by", "grp"),
            P("bx", "by", None, "grp"),
            P("bx", "by", None, "grp"),
            P("bx", "by", "grp"),
            P(None, "bx", "by", None, "grp"),
            P("bx", "by", None, "grp"),
        ),
        out_specs=(P(None, "bx", "by", "grp"), P("grp")),
        check_vma=False,
    )
```

profile of v0, /device:TPU:0, one launch (start us, length us, event | category | flops | bytes accessed | tf_op | source)
XLA Modules:
  0.0 87.8 jit_solution(11073613806493202705)
XLA Ops:
  0.6 0.8 copy.16
  1.5 0.0 copy-start
  1.5 1.7 %copy-done = bf16[302,1,1,32,128]{4,3,2,1,0:T(8,128)(2,1)S(1)} copy-done((bf16[302,1,1,32,128]{4,3,2,1,0:T(8,128)(2,1)S(1)}, bf16[302,1,1,32,128]{4,3,2,1,0:T(8,128)(2,1)}, u32[]{:S(2)}) %copy-start) | copy-done | bytes 2474008
  3.2 0.0 copy-start.1
  3.2 0.7 copy-done.1
  3.9 0.0 copy-start.2
  3.9 0.7 copy-done.2
  4.6 0.0 copy-start.3
  4.6 0.7 copy-done.3
  5.3 0.0 copy-start.4
  5.3 0.7 copy-done.4
  6.0 0.0 copy-start.5
  6.0 0.9 %copy-done.5 = bf16[128,912]{1,0:T(8,128)(2,1)S(1)} copy-done((bf16[128,912]{1,0:T(8,128)(2,1)S(1)}, bf16[128,912]{1,0:T(8,128)(2,1)}, u32[]{:S(2)}) %copy-start.5) | copy-done | bytes 233496
  6.9 0.0 copy-start.6
  6.9 0.9 %copy-done.6 = bf16[304,384]{1,0:T(8,128)(2,1)S(1)} copy-done((bf16[304,384]{1,0:T(8,128)(2,1)S(1)}, bf16[304,384]{1,0:T(8,128)(2,1)}, u32[]{:S(2)}) %copy-start.6) | copy-done | bytes 233496
  7.9 0.0 copy-start.7
  7.9 0.8 copy-done.7
  8.7 0.0 copy-start.8
  8.7 0.8 copy-done.8
  9.5 77.0 %shard_map.113 = (f32[121,128]{1,0:T(8,128)S(1)}, f32[8,128]{1,0:T(8,128)S(1)}) custom-call(f32[121,128]{1,0:T(8,128)S(1)} %bitcast.10, s32[32,128]{1,0:T(8,128)S(1)} %bitcast.12, s32[32,128]{1,0:T(8,128)S(1)} %bitcast.13, s32[1,128]{1,0:T(1,128)S(1)} %bitcast.15, bf16[302,32,128]{2,1,0:T(8,128)(2,1)S(1)} %bitcast.11, f32[32,128]{1,0:T(8,128)S(1)} %bitcast.14, ...), custom_call_target="tpu_custom_call" | custom-call | flops 12985565184 | bytes 4194304 | tf_op jit(solution)/shard_map/pallas_call | solution.py:287
  86.5 0.7 copy.13
  87.2 0.6 slice_reduce_fusion
Async XLA Ops:
  1.5 1.7 %copy-start = (bf16[302,1,1,32,128]{4,3,2,1,0:T(8,128)(2,1)S(1)}, bf16[302,1,1,32,128]{4,3,2,1,0:T(8,128)(2,1)}, u32[]{:S(2)}) copy-start(bf16[302,1,1,32,128]{4,3,2,1,0:T(8,128)(2,1)} %param.14) | copy-start | bytes 7421956
  3.2 0.7 copy-start.1
  3.9 0.7 copy-start.2
  4.6 0.7 copy-start.3
  5.3 0.7 copy-start.4
  6.0 0.9 %copy-start.5 = (bf16[128,912]{1,0:T(8,128)(2,1)S(1)}, bf16[128,912]{1,0:T(8,128)(2,1)}, u32[]{:S(2)}) copy-start(bf16[128,912]{1,0:T(8,128)(2,1)} %constant.9.clone.bt_ref) | copy-start | bytes 700420
  6.9 0.9 %copy-start.6 = (bf16[304,384]{1,0:T(8,128)(2,1)S(1)}, bf16[304,384]{1,0:T(8,128)(2,1)}, u32[]{:S(2)}) copy-start(bf16[304,384]{1,0:T(8,128)(2,1)} %constant.8.clone.bc_ref) | copy-start | bytes 700420
  7.9 0.8 copy-start.7
  8.7 0.8 copy-start.8
where the time goes:
time: 88.3 us; the launch traced here: 87.8 us
  Pallas kernels  77 us (87%)
  local copies, waits for them, and re-layouts  10.2 us (12%)
    pallas_call x1, Pallas kernels, on_device(): pl.pallas_call(functools.partial(kernel, nbx, nby, cells), out_shape=(jax...  77 us
    unnamed x20, local copies, waits for them, and re-layouts  9.59 us

commit v1 on v0

--- a/solution.py
+++ b/solution.py
@@ -13,7 +13,7 @@
 MESH = pl.DeviceIdType.MESH
 GOLDEN = 2.399963229728653
 HP = 128
-WIDE = 2
+WIDE = 8
 BF = jnp.bfloat16
 F32 = jnp.float32
 
@@ -51,28 +51,29 @@
     return np.stack(columns, axis=1)
 
 
-def split_np(x):
-    hi = x.astype(np.float32).astype(BF)
-    lo = (x - hi.astype(np.float64)).astype(np.float32).astype(BF)
-    return hi, lo
-
-
 def kernel(
     nbx, nby, cells,
-    psi_ref, nblk_ref, nsph_ref, cnt_ref, couple_ref, ratio_ref, bc_ref, bt_ref, deg_ref, invd_ref,
+    psi_hbm, nblk_hbm, nsph_hbm, cnt_hbm, couple_hbm, ratio_hbm, basis_hbm, basist_hbm,
     out_ref, norm_ref,
-    cin, cf, cd, onehot, power, land, solcat, sol0, nb, nland1, nland2,
+    psi_ref, nblk_ref, nsph_ref, cnt_ref, cin, ratio_ref, basis_ref, basist_ref,
+    bc_ref, bt_ref, cf, cd, onehot, power, land, solcat, sol0, nb, nland1, nland2,
     csem, ssem, rsem, s1, r1, s2, r2,
 ):
     lh, sph = psi_ref.shape
-    npts, slots, _ = couple_ref.shape
-    npad = bc_ref.shape[0]
+    npts, slots, _ = cin.shape
+    npad = basis_ref.shape[0]
     groups = slots // WIDE
     wide = WIDE * sph
     ix, iy, ig = lax.axis_index("bx"), lax.axis_index("by"), lax.axis_index("grp")
 
-    copy_in = pltpu.make_async_copy(couple_ref, cin, csem)
-    copy_in.start()
+    sources = (psi_hbm, nblk_hbm, nsph_hbm, cnt_hbm, ratio_hbm, basis_hbm, basist_hbm, couple_hbm)
+    places = (psi_ref, nblk_ref, nsph_ref, cnt_ref, ratio_ref, basis_ref, basist_ref, cin)
+    loads = [
+        pltpu.make_async_copy(source, target, csem.at[i])
+        for i, (source, target) in enumerate(zip(sources, places))
+    ]
+    for load in loads:
+        load.start()
 
     dirs = [d for d in range(9) if d != 4]
     inside = {}
@@ -110,8 +111,14 @@
         def _(peer=peer):
             pl.semaphore_signal(barrier, inc=1, device_id=(ig, peer, iy), device_id_type=MESH)
 
+    row = lax.broadcasted_iota(jnp.int32, (HP, sph), 0)
+    degree = jnp.zeros((HP, sph), F32)
+    for level in range(1, math.isqrt(lh)):
+        degree = degree + (row >= level * level).astype(F32)
+    inverse = jnp.where(row < lh, (2.0 * degree + 1.0) * (1.0 / (4.0 * math.pi)), 0.0)
     sol0[...] = jnp.zeros_like(sol0)
-    sol0[pl.ds(0, lh), :] = psi_ref[...] * invd_ref[pl.ds(0, lh), :]
+    loads[0].wait()
+    sol0[pl.ds(0, lh), :] = psi_ref[...] * inverse[:lh]
     land[0, 4] = sol0[...]
     pl.semaphore_wait(barrier, count)
 
@@ -149,6 +156,8 @@
 
     send_all(0)
 
+    for load in loads[1:7]:
+        load.wait()
     rows = lax.broadcasted_iota(jnp.int32, (9 * sph, sph), 0)
 
     def prepare(g, carry):
@@ -158,13 +167,24 @@
             index = nblk_ref[pl.ds(s, 1), :] * sph + nsph_ref[pl.ds(s, 1), :]
             onehot[g, :, lanes] = (rows == index).astype(F32).astype(BF)
             logr = jnp.log(ratio_ref[pl.ds(s, 1), :])
-            raised = jnp.exp(deg_ref[...] * logr) * invd_ref[...]
+            raised = jnp.exp(degree * logr) * inverse
             power[g, :, lanes] = jnp.where(s < cnt_ref[...], raised, 0.0)
         return carry
 
     lax.fori_loop(0, groups, prepare, 0)
 
-    copy_in.wait()
+    quad = 4.0 * math.pi / npts
+    for source, target, width, scale in (
+        (basis_ref, bc_ref, HP, quad),
+        (basist_ref, bt_ref, npad, 1.0),
+    ):
+        value = source[...] * scale
+        hi = value.astype(BF)
+        target[:, pl.ds(0, width)] = hi
+        target[:, pl.ds(width, width)] = hi
+        target[:, pl.ds(2 * width, width)] = (value - hi.astype(F32)).astype(BF)
+
+    loads[7].wait()
 
     def widen(n, carry):
         cf[pl.ds(n * slots, slots), :] = cin[n].astype(F32)
@@ -271,16 +291,6 @@
     npad = -(-npts // 16) * 16
     basis = np.zeros((npad, HP))
     basis[:npts, :lh] = basis_table(npts, lmax)
-    degrees = np.zeros((HP,))
-    degrees[:lh] = np.repeat(np.arange(lmax + 1), 2 * np.arange(lmax + 1) + 1)
-    inverse = (2.0 * degrees + 1.0) / (4.0 * math.pi)
-    inverse[lh:] = 0.0
-    hi, lo = split_np(basis * (4.0 * math.pi / npts))
-    bc = np.concatenate([hi, hi, lo], axis=1)
-    hi, lo = split_np(basis.T)
-    bt = np.concatenate([hi, hi, lo], axis=1)
-    deg = np.broadcast_to(degrees[:, None], (HP, sph)).astype(np.float32)
-    invd = np.broadcast_to(inverse[:, None], (HP, sph)).astype(np.float32)
     cells = lh * sph * nbx * nby
     groups = slots // WIDE
     vmem = pl.BlockSpec(memory_space=pltpu.VMEM)
@@ -290,10 +300,19 @@
             jax.ShapeDtypeStruct((lh, sph), F32),
             jax.ShapeDtypeStruct((8, 128), F32),
         ),
-        in_specs=[vmem] * 4 + [pl.BlockSpec(memory_space=pl.ANY)] + [vmem] * 5,
+        in_specs=[pl.BlockSpec(memory_space=pltpu.HBM)] * 8,
         out_specs=(vmem, vmem),
         scratch_shapes=[
+            pltpu.VMEM((lh, sph), F32),
+            pltpu.VMEM((slots, sph), jnp.int32),
+            pltpu.VMEM((slots, sph), jnp.int32),
+            pltpu.VMEM((1, sph), jnp.int32),
             pltpu.VMEM((npts, slots, sph), BF),
+            pltpu.VMEM((slots, sph), F32),
+            pltpu.VMEM((npad, HP), F32),
+            pltpu.VMEM((HP, npad), F32),
+            pltpu.VMEM((npad, 3 * HP), BF),
+            pltpu.VMEM((HP, 3 * npad), BF),
             pltpu.VMEM((npad * slots, sph), F32),
             pltpu.VMEM((groups, npad, WIDE * sph), F32),
             pltpu.VMEM((groups, 9 * sph, WIDE * sph), BF),
@@ -304,7 +323,7 @@
             pltpu.VMEM((8, sph), F32),
             pltpu.VMEM((nby, 8, sph), F32),
             pltpu.VMEM((nbx, 8, sph), F32),
-            pltpu.SemaphoreType.DMA(()),
+            pltpu.SemaphoreType.DMA((8,)),
             pltpu.SemaphoreType.DMA((SWEEPS, 9)),
             pltpu.SemaphoreType.DMA((SWEEPS, 9)),
             pltpu.SemaphoreType.DMA((nby,)),
@@ -313,7 +332,7 @@
             pltpu.SemaphoreType.DMA((nbx,)),
         ],
         compiler_params=pltpu.CompilerParams(
-            collective_id=0, has_side_effects=True, vmem_limit_bytes=48 * 1024 * 1024
+            collective_id=0, has_side_effects=True, vmem_limit_bytes=63 * 1024 * 1024
         ),
         cost_estimate=pl.CostEstimate(
             flops=2 * SWEEPS * slots * sph * (2304 * HP + 6 * npad * HP),
@@ -327,10 +346,8 @@
         counts.reshape(1, sph),
         couple.reshape(npts, slots, sph),
         ratio.reshape(slots, sph),
-        jnp.asarray(bc),
-        jnp.asarray(bt),
-        jnp.asarray(deg),
-        jnp.asarray(invd),
+        jnp.asarray(basis.astype(np.float32)),
+        jnp.asarray(basis.T.astype(np.float32)),
     )
     return out.reshape(lh, 1, 1, sph), norms[:SWEEPS, 0]
 

time: 88.3 us -> 54 us (0.61)
  Pallas kernels: 77 us -> 48.8 us
  local copies, waits for them, and re-layouts: 10.2 us -> 4.28 us
    pallas_call x1, Pallas kernels: 77 us -> 48.8 us  [on_device(): pl.pallas_call(functools.partial(kernel, nbx, nby, cells), out_shape=(jax...]
    unnamed x20 -> x2, local copies, waits for them, and re-layouts: 9.59 us -> 2.98 us
where the time goes in v1:
time: 54 us; the launch traced here: 53.7 us
  Pallas kernels  48.8 us (90%)
  local copies, waits for them, and re-layouts  4.28 us (8%)
  between operations  0.64 us (1%)
    pallas_call x1, Pallas kernels, on_device(): pl.pallas_call(functools.partial(kernel, nbx, nby, cells), out_shape=(jax...  48.8 us
    unnamed x2, local copies, waits for them, and re-layouts  2.98 us
    slice x1, local copies, waits for them, and re-layouts, on_device(): return (out.reshape(lh, 1, 1, sph), norms[:SWEEPS, 0])  1.3 us

profile of v1, /device:TPU:0, one launch (start us, length us, event | category | flops | bytes accessed | tf_op | source)
XLA Modules:
  0.0 53.7 jit_solution(6148881858905642447)
XLA Ops:
  0.6 1.5 %copy.14 = f32[121,1,1,128]{3,0,1,2:T(8,128)} copy(f32[121,1,1,128]{3,2,1,0:T(1,128)} %param.8) | data formatting | bytes 123904
  2.1 48.8 %shard_map.95 = (f32[121,128]{1,0:T(8,128)}, f32[8,128]{1,0:T(8,128)}) custom-call(f32[121,128]{1,0:T(8,128)} %bitcast.10, s32[32,128]{1,0:T(8,128)} %bitcast.12, s32[32,128]{1,0:T(8,128)} %bitcast.13, s32[1,128]{1,0:T(1,128)} %bitcast.15, bf16[302,32,128]{2,1,0:T(8,128)(2,1)} %bitcast.11, f32[32,128]{1,0:T(8,128)} %bitcast.14, ...), custom_call_target="tpu_custom_call" | custom-call | flops 12985565184 | bytes 4194304 | tf_op jit(solution)/shard_map/pallas_call | solution.py:297
  50.9 1.5 %copy.11 = f32[121,1,1,128]{3,2,1,0:T(1,128)} copy(f32[121,1,1,128]{3,0,2,1:T(8,128)} %bitcast.9) | data formatting | bytes 123904
  52.4 1.3 %slice_reduce_fusion = f32[3]{0:T(128)} fusion(f32[8,128]{1,0:T(8,128)} %get-tuple-element.5), kind=kLoop, calls=%fused_computation.1 | loop fusion | bytes 24 | tf_op jit(solution)/shard_map/slice | solution.py:352

commit v2 on v1

--- a/solution.py
+++ b/solution.py
@@ -14,6 +14,9 @@
 GOLDEN = 2.399963229728653
 HP = 128
 WIDE = 8
+DIRECT = 32
+ORDER = (4, 3, 5, 1, 7, 0, 2, 6, 8)
+EARLY = 5
 BF = jnp.bfloat16
 F32 = jnp.float32
 
@@ -56,10 +59,10 @@
     psi_hbm, nblk_hbm, nsph_hbm, cnt_hbm, couple_hbm, ratio_hbm, basis_hbm, basist_hbm,
     out_ref, norm_ref,
     psi_ref, nblk_ref, nsph_ref, cnt_ref, cin, ratio_ref, basis_ref, basist_ref,
-    bc_ref, bt_ref, cf, cd, onehot, power, land, solcat, sol0, nb, nland1, nland2,
+    bc_ref, bt_ref, cf, cd, picked, onehot, power, land, solcat, sol0, nb, nland1, nland2,
     csem, ssem, rsem, s1, r1, s2, r2,
 ):
-    lh, sph = psi_ref.shape
+    lh, _, sph = psi_ref.shape
     npts, slots, _ = cin.shape
     npad = basis_ref.shape[0]
     groups = slots // WIDE
@@ -75,7 +78,7 @@
     for load in loads:
         load.start()
 
-    dirs = [d for d in range(9) if d != 4]
+    dirs = ORDER[1:]
     inside = {}
     for d in dirs:
         tx, ty = ix + d // 3 - 1, iy + d % 3 - 1
@@ -85,31 +88,45 @@
         return (ig, ix + d // 3 - 1, iy + d % 3 - 1)
 
     barrier = pltpu.get_barrier_semaphore()
-    count = jnp.int32(0)
-    for d in dirs:
-        count = count + inside[d].astype(jnp.int32)
-
-        @pl.when(inside[d])
-        def _(d=d):
-            pl.semaphore_signal(barrier, inc=1, device_id=device(d), device_id_type=MESH)
-
-    for off in range(1, nby):
-        peer = lax.rem(iy + off, nby)
-        far = jnp.abs(peer - iy) >= 2
-        count = count + far.astype(jnp.int32)
-
-        @pl.when(far)
-        def _(peer=peer):
-            pl.semaphore_signal(barrier, inc=1, device_id=(ig, ix, peer), device_id_type=MESH)
-
-    for off in range(1, nbx):
-        peer = lax.rem(ix + off, nbx)
-        far = jnp.abs(peer - ix) >= 2
-        count = count + far.astype(jnp.int32)
-
-        @pl.when(far)
-        def _(peer=peer):
-            pl.semaphore_signal(barrier, inc=1, device_id=(ig, peer, iy), device_id_type=MESH)
+    ranks = nbx * nby
+    me = ix * nby + iy
+    direct = ranks <= DIRECT
+
+    def member(peer):
+        return (ig, lax.div(peer, nby), lax.rem(peer, nby))
+
+    if direct:
+        for off in range(1, ranks):
+            pl.semaphore_signal(
+                barrier, inc=1, device_id=member(lax.rem(me + off, ranks)), device_id_type=MESH
+            )
+        count = ranks - 1
+    else:
+        count = jnp.int32(0)
+        for d in dirs:
+            count = count + inside[d].astype(jnp.int32)
+
+            @pl.when(inside[d])
+            def _(d=d):
+                pl.semaphore_signal(barrier, inc=1, device_id=device(d), device_id_type=MESH)
+
+        for off in range(1, nby):
+            peer = lax.rem(iy + off, nby)
+            far = jnp.abs(peer - iy) >= 2
+            count = count + far.astype(jnp.int32)
+
+            @pl.when(far)
+            def _(peer=peer):
+                pl.semaphore_signal(barrier, inc=1, device_id=(ig, ix, peer), device_id_type=MESH)
+
+        for off in range(1, nbx):
+            peer = lax.rem(ix + off, nbx)
+            far = jnp.abs(peer - ix) >= 2
+            count = count + far.astype(jnp.int32)
+
+            @pl.when(far)
+            def _(peer=peer):
+                pl.semaphore_signal(barrier, inc=1, device_id=(ig, peer, iy), device_id_type=MESH)
 
     row = lax.broadcasted_iota(jnp.int32, (HP, sph), 0)
     degree = jnp.zeros((HP, sph), F32)
@@ -118,7 +135,7 @@
     inverse = jnp.where(row < lh, (2.0 * degree + 1.0) * (1.0 / (4.0 * math.pi)), 0.0)
     sol0[...] = jnp.zeros_like(sol0)
     loads[0].wait()
-    sol0[pl.ds(0, lh), :] = psi_ref[...] * inverse[:lh]
+    sol0[pl.ds(0, lh), :] = psi_ref[...].reshape(lh, sph) * inverse[:lh]
     land[0, 4] = sol0[...]
     pl.semaphore_wait(barrier, count)
 
@@ -151,20 +168,24 @@
     def place(block, d):
         hi = block.astype(BF)
         lo = (block - hi.astype(F32)).astype(BF)
-        solcat[pl.ds(0, HP), pl.ds(d * sph, sph)] = hi
-        solcat[pl.ds(HP, HP), pl.ds(d * sph, sph)] = lo
+        solcat[pl.ds(0, HP), pl.ds(ORDER.index(d) * sph, sph)] = hi
+        solcat[pl.ds(HP, HP), pl.ds(ORDER.index(d) * sph, sph)] = lo
 
     send_all(0)
 
     for load in loads[1:7]:
         load.wait()
     rows = lax.broadcasted_iota(jnp.int32, (9 * sph, sph), 0)
+    position = jnp.zeros((slots, sph), jnp.int32)
+    for at, d in enumerate(ORDER):
+        position = jnp.where(nblk_ref[...] == d, at, position)
+    nblk_ref[...] = position * sph + nsph_ref[...]
 
     def prepare(g, carry):
         for w in range(WIDE):
             s = g * WIDE + w
             lanes = pl.ds(w * sph, sph)
-            index = nblk_ref[pl.ds(s, 1), :] * sph + nsph_ref[pl.ds(s, 1), :]
+            index = nblk_ref[pl.ds(s, 1), :]
             onehot[g, :, lanes] = (rows == index).astype(F32).astype(BF)
             logr = jnp.log(ratio_ref[pl.ds(s, 1), :])
             raised = jnp.exp(degree * logr) * inverse
@@ -200,24 +221,47 @@
 
     lax.fori_loop(0, groups, turn, 0)
 
+    def arrive(t, blocks):
+        for d in blocks:
+            @pl.when(inside[d])
+            def _(d=d, t=t):
+                block_arrival(t, d).wait_recv()
+                place(land[t, d], d)
+
+            if t == 0:
+                @pl.when(jnp.logical_not(inside[d]))
+                def _(d=d):
+                    solcat[:, pl.ds(ORDER.index(d) * sph, sph)] = jnp.zeros((2 * HP, sph), BF)
+
+    early = EARLY * sph
+
+    def pick_early(g, carry):
+        picked[g] = jnp.dot(
+            solcat[:, pl.ds(0, early)], onehot[g, pl.ds(0, early), :], preferred_element_type=F32
+        ).astype(BF)
+        return carry
+
+    def pick_late(g, carry):
+        rest = jnp.dot(
+            solcat[:, pl.ds(early, 9 * sph - early)],
+            onehot[g, pl.ds(early, 9 * sph - early), :],
+            preferred_element_type=F32,
+        )
+        picked[g] = (picked[g].astype(F32) + rest).astype(BF)
+        return carry
+
     nb[...] = jnp.zeros_like(nb)
     for t in range(SWEEPS):
         old = land[t, 4]
         place(old, 4)
-        for d in dirs:
-            @pl.when(inside[d])
-            def _(d=d, t=t):
-                block_arrival(t, d).wait_recv()
-                place(land[t, d], d)
-
-            if t == 0:
-                @pl.when(jnp.logical_not(inside[d]))
-                def _(d=d):
-                    solcat[:, pl.ds(d * sph, sph)] = jnp.zeros((2 * HP, sph), BF)
+        arrive(t, ORDER[1:EARLY])
+        lax.fori_loop(0, groups, pick_early, 0, unroll=2)
+        arrive(t, ORDER[EARLY:])
+        lax.fori_loop(0, groups, pick_late, 0, unroll=2)
 
         def pairs(g, total):
-            picked = jnp.dot(solcat[...], onehot[g], preferred_element_type=F32).astype(BF)
-            stacked = jnp.concatenate([picked, picked[:HP]], axis=0)
+            chosen = picked[g]
+            stacked = jnp.concatenate([chosen, chosen[:HP]], axis=0)
             points = jnp.dot(bc_ref[...], stacked, preferred_element_type=F32)
             product = points * cd[g]
             hi = product.astype(BF)
@@ -271,8 +315,11 @@
             copy.wait_send()
         return result
 
-    part = reduce_line(nb[...], nland1, s1, r1, iy, nby, lambda p: (ig, ix, p))
-    part = reduce_line(part, nland2, s2, r2, ix, nbx, lambda p: (ig, p, iy))
+    if direct:
+        part = reduce_line(nb[...], nland1, s1, r1, me, ranks, member)
+    else:
+        part = reduce_line(nb[...], nland1, s1, r1, iy, nby, lambda p: (ig, ix, p))
+        part = reduce_line(part, nland2, s2, r2, ix, nbx, lambda p: (ig, p, iy))
     norm = jnp.sqrt(jnp.sum(part, axis=1, keepdims=True) * (1.0 / cells))
     norm_ref[...] = jnp.broadcast_to(norm, norm_ref.shape)
 
@@ -293,6 +340,7 @@
     basis[:npts, :lh] = basis_table(npts, lmax)
     cells = lh * sph * nbx * nby
     groups = slots // WIDE
+    line = nbx * nby if nbx * nby <= DIRECT else nby
     vmem = pl.BlockSpec(memory_space=pltpu.VMEM)
     out, norms = pl.pallas_call(
         functools.partial(kernel, nbx, nby, cells),
@@ -303,7 +351,7 @@
         in_specs=[pl.BlockSpec(memory_space=pltpu.HBM)] * 8,
         out_specs=(vmem, vmem),
         scratch_shapes=[
-            pltpu.VMEM((lh, sph), F32),
+            pltpu.VMEM((lh, 1, sph), F32),
             pltpu.VMEM((slots, sph), jnp.int32),
             pltpu.VMEM((slots, sph), jnp.int32),
             pltpu.VMEM((1, sph), jnp.int32),
@@ -315,19 +363,20 @@
             pltpu.VMEM((HP, 3 * npad), BF),
             pltpu.VMEM((npad * slots, sph), F32),
             pltpu.VMEM((groups, npad, WIDE * sph), F32),
+            pltpu.VMEM((groups, 2 * HP, WIDE * sph), BF),
             pltpu.VMEM((groups, 9 * sph, WIDE * sph), BF),
             pltpu.VMEM((groups, HP, WIDE * sph), F32),
             pltpu.VMEM((SWEEPS, 9, HP, sph), F32),
             pltpu.VMEM((2 * HP, 9 * sph), BF),
             pltpu.VMEM((HP, sph), F32),
             pltpu.VMEM((8, sph), F32),
-            pltpu.VMEM((nby, 8, sph), F32),
+            pltpu.VMEM((line, 8, sph), F32),
             pltpu.VMEM((nbx, 8, sph), F32),
             pltpu.SemaphoreType.DMA((8,)),
             pltpu.SemaphoreType.DMA((SWEEPS, 9)),
             pltpu.SemaphoreType.DMA((SWEEPS, 9)),
-            pltpu.SemaphoreType.DMA((nby,)),
-            pltpu.SemaphoreType.DMA((nby,)),
+            pltpu.SemaphoreType.DMA((line,)),
+            pltpu.SemaphoreType.DMA((line,)),
             pltpu.SemaphoreType.DMA((nbx,)),
             pltpu.SemaphoreType.DMA((nbx,)),
         ],
@@ -340,7 +389,7 @@
             transcendentals=slots * sph * HP,
         ),
     )(
-        psi.reshape(lh, sph),
+        psi.reshape(lh, 1, sph),
         nbr_block.reshape(slots, sph),
         nbr_sphere.reshape(slots, sph),
         counts.reshape(1, sph),

time: 54 us -> 50.7 us (0.939)
  Pallas kernels: 48.8 us -> 47 us
  local copies, waits for them, and re-layouts: 4.28 us -> 2.83 us
    pallas_call x1, Pallas kernels: 48.8 us -> 47 us  [on_device(): pl.pallas_call(functools.partial(kernel, nbx, nby, cells), out_shape=(jax...]
    unnamed x2 -> x1, local copies, waits for them, and re-layouts: 2.98 us -> 1.53 us
where the time goes in v2:
time: 50.7 us; the launch traced here: 50.5 us
  Pallas kernels  47 us (93%)
  local copies, waits for them, and re-layouts  2.83 us (6%)
  between operations  0.64 us (1%)
    pallas_call x1, Pallas kernels, on_device(): pl.pallas_call(functools.partial(kernel, nbx, nby, cells), out_shape=(jax...  47 us
    unnamed x1, local copies, waits for them, and re-layouts  1.53 us
    slice x1, local copies, waits for them, and re-layouts, on_device(): return (out.reshape(lh, 1, 1, sph), norms[:SWEEPS, 0])  1.3 us

profile of v2, /device:TPU:0, one launch (start us, length us, event | category | flops | bytes accessed | tf_op | source)
XLA Modules:
  0.0 50.5 jit_solution(6708317941641073742)
XLA Ops:
  0.6 47.0 %shard_map.95 = (f32[121,128]{1,0:T(8,128)}, f32[8,128]{1,0:T(8,128)}) custom-call(f32[121,1,128]{2,1,0:T(1,128)} %bitcast.9, s32[32,128]{1,0:T(8,128)} %bitcast.10, s32[32,128]{1,0:T(8,128)} %bitcast.11, s32[1,128]{1,0:T(1,128)} %bitcast.13, bf16[302,32,128]{2,1,0:T(8,128)(2,1)} %bitcast.8, f32[32,128]{1,0:T(8,128)} %bitcast.12, ...), custom_call_target="tpu_custom_call" | custom-call | flops 12985565184 | bytes 4194304 | tf_op jit(solution)/shard_map/pallas_call | solution.py:345
  47.7 1.5 %copy.11 = f32[121,1,1,128]{3,2,1,0:T(1,128)} copy(f32[121,1,1,128]{3,0,2,1:T(8,128)} %bitcast.7) | data formatting | bytes 123904
  49.2 1.3 %slice_reduce_fusion = f32[3]{0:T(128)} fusion(f32[8,128]{1,0:T(8,128)} %get-tuple-element.5), kind=kLoop, calls=%fused_computation | loop fusion | bytes 24 | tf_op jit(solution)/shard_map/slice | solution.py:401

commit v3 on v2

--- a/solution.py
+++ b/solution.py
@@ -274,7 +274,7 @@
                 total = total + terms[:, w * sph:(w + 1) * sph]
             return total
 
-        total = lax.fori_loop(0, groups, pairs, jnp.zeros((HP, sph), F32), unroll=2)
+        total = lax.fori_loop(0, groups, pairs, jnp.zeros((HP, sph), F32), unroll=4)
         fresh = sol0[...] - total
         if t < SWEEPS - 1:
             land[t + 1, 4] = fresh

time: 50.7 us -> 50 us (0.986)
  Pallas kernels: 47 us -> 46.4 us
    pallas_call x1, Pallas kernels: 47 us -> 46.4 us  [on_device(): pl.pallas_call(functools.partial(kernel, nbx, nby, cells), out_shape=(jax...]
where the time goes in v3:
time: 50 us; the launch traced here: 49.8 us
  Pallas kernels  46.4 us (93%)
  local copies, waits for them, and re-layouts  2.83 us (6%)
  between operations  0.64 us (1%)
    pallas_call x1, Pallas kernels, on_device(): pl.pallas_call(functools.partial(kernel, nbx, nby, cells), out_shape=(jax...  46.4 us
    unnamed x1, local copies, waits for them, and re-layouts  1.53 us
    slice x1, local copies, waits for them, and re-layouts, on_device(): return (out.reshape(lh, 1, 1, sph), norms[:SWEEPS, 0])  1.3 us

profile of v3, /device:TPU:0, one launch (start us, length us, event | category | flops | bytes accessed | tf_op | source)
XLA Modules:
  0.0 49.8 jit_solution(14364568213317336614)
XLA Ops:
  0.6 46.4 %shard_map.95 = (f32[121,128]{1,0:T(8,128)}, f32[8,128]{1,0:T(8,128)}) custom-call(f32[121,1,128]{2,1,0:T(1,128)} %bitcast.9, s32[32,128]{1,0:T(8,128)} %bitcast.10, s32[32,128]{1,0:T(8,128)} %bitcast.11, s32[1,128]{1,0:T(1,128)} %bitcast.13, bf16[302,32,128]{2,1,0:T(8,128)(2,1)} %bitcast.8, f32[32,128]{1,0:T(8,128)} %bitcast.12, ...), custom_call_target="tpu_custom_call" | custom-call | flops 12985565184 | bytes 4194304 | tf_op jit(solution)/shard_map/pallas_call | solution.py:345
  47.0 1.5 %copy.11 = f32[121,1,1,128]{3,2,1,0:T(1,128)} copy(f32[121,1,1,128]{3,0,2,1:T(8,128)} %bitcast.7) | data formatting | bytes 123904
  48.5 1.3 %slice_reduce_fusion = f32[3]{0:T(128)} fusion(f32[8,128]{1,0:T(8,128)} %get-tuple-element.5), kind=kLoop, calls=%fused_computation | loop fusion | bytes 24 | tf_op jit(solution)/shard_map/slice | solution.py:401
